TPU v7x, 32 devices: a whole 2x2x4 slice. The times are simulated.
32 devices in a mesh: gx: 4 (over z), gy: 4 (over y, x), gz: 2 (over core).
Axes of the slice: x: 2, y: 2, z: 4, core: 2. Of those that a mesh axis runs over, the one named last changes fastest.
Arguments:
- source: bfloat16 [32, 1024, 1024], P('gx', 'gy', 'gz'), may hold values from -14 to 14
- observed: bfloat16 [32, 1024, 1024], P('gx', 'gy', 'gz'), may hold values from -14 to 14
- physics: float32 [3], replicated, may hold values from -8.5 to 0.5, as said below
- first_weight: float32 [3, 256], replicated, may hold values from -12 to 12
- first_bias: float32 [3, 256], replicated, may hold values from -8 to 8
- hidden_weight: float32 [3, 2, 256, 256], replicated, may hold values from -0.45 to 0.45
- hidden_bias: float32 [3, 2, 256], replicated, may hold values from -3 to 3
- final_weight: float32 [3, 256, 64], replicated, may hold values from -0.375 to 0.375
- final_bias: float32 [3, 64], replicated, may hold values from -3 to 3
Outputs:
- total_loss: float32 [], replicated
- physics_grad: float32 [3], replicated
- first_weight_grad: float32 [3, 256], replicated
- first_bias_grad: float32 [3, 256], replicated
- hidden_weight_grad: float32 [3, 2, 256, 256], replicated
- hidden_bias_grad: float32 [3, 2, 256], replicated
- final_weight_grad: float32 [3, 256, 64], replicated
- final_bias_grad: float32 [3, 64], replicated
Inputs may be any that keep to these rules, and one draw needn't show every extreme that they name: physics[0] lies in -8.5 .. -7.0, physics[1] in 0.04 .. 0.16, physics[2] in -0.5 .. 0.5.
All inputs are finite; a program needn't handle non-finite values.
Results may differ from a plain program's by a relative error of at most 0.0003.
Values sent between devices are 32-bit elements; how exact they have to be, the bound alone decides.
A program may use at most 128 MiB of HBM per device.

v0:
```python
import functools
import jax
import jax.numpy as jnp
from jax import lax
from jax.experimental import pallas as pl
from jax.experimental.pallas import tpu as pltpu
from jax.sharding import PartitionSpec as P

HIGHEST = lax.Precision.HIGHEST
CHUNK = 128

LANES = 256
MESH_ID = pl.DeviceIdType.MESH


def reduce_plan(total_rows, sizes):
    devices = 1
    for size in sizes.values():
        devices *= size
    unit = 8 * devices
    units = -(-total_rows // unit)
    lead = max(1, (units * 7 + 5) // 10)
    if lead == units and units > 1:
        lead -= 1
    channels = [(0, lead * unit, ("gz", "gy", "gx"))]
    if units > lead:
        channels.append((lead * unit, (units - lead) * unit, ("gz", "gx", "gy")))
    return units * unit, channels


def all_reduce_body(channels, sizes, in_ref, out_ref, recv_refs, work_refs, sems):
    places = {name: lax.axis_index(name) for name in sizes}

    def partner(name, step):
        return {name: lax.rem(places[name] + step, sizes[name])}

    phases = len(sizes)
    sources = [in_ref] * len(channels)
    starts = [first for first, _, _ in channels]
    lengths = [rows for _, rows, _ in channels]
    bases = [first for first, _, _ in channels]
    history = [[] for _ in channels]
    for phase in range(phases):
        flights = []
        for slot, (_, _, order) in enumerate(channels):
            name = order[phase]
            part = lengths[slot] // sizes[name]
            for step in range(1, sizes[name]):
                peer = lax.rem(places[name] + step, sizes[name])
                copy = pltpu.make_async_remote_copy(
                    src_ref=sources[slot].at[pl.ds(pl.multiple_of(starts[slot] + peer * part, 8), part)],
                    dst_ref=recv_refs[slot][phase].at[step - 1],
                    send_sem=sems[slot][0].at[phase, step - 1],
                    recv_sem=sems[slot][1].at[phase, step - 1],
                    device_id=partner(name, step),
                    device_id_type=MESH_ID,
                )
                copy.start()
                flights.append((slot, copy))
        for slot, (_, _, order) in enumerate(channels):
            name = order[phase]
            part = lengths[slot] // sizes[name]
            for owner, copy in flights:
                if owner == slot:
                    copy.wait()
            mine = pl.multiple_of(starts[slot] + places[name] * part, 8)
            value = sources[slot][pl.ds(mine, part)]
            for step in range(1, sizes[name]):
                value = value + recv_refs[slot][phase][step - 1]
            history[slot].append((name, bases[slot], part))
            bases[slot] = pl.multiple_of(bases[slot] + places[name] * part, 8)
            if phase == phases - 1:
                out_ref[pl.ds(bases[slot], part)] = value
            else:
                work_refs[slot][phase][...] = value
                sources[slot] = work_refs[slot][phase]
                starts[slot] = 0
            lengths[slot] = part
    for phase in reversed(range(phases)):
        flights = []
        for slot in range(len(channels)):
            name, base, part = history[slot][phase]
            mine = out_ref.at[pl.ds(pl.multiple_of(base + places[name] * part, 8), part)]
            for step in range(1, sizes[name]):
                copy = pltpu.make_async_remote_copy(
                    src_ref=mine,
                    dst_ref=mine,
                    send_sem=sems[slot][2].at[phase, step - 1],
                    recv_sem=sems[slot][3].at[phase, step - 1],
                    device_id=partner(name, step),
                    device_id_type=MESH_ID,
                )
                copy.start()
                flights.append(copy)
        for copy in flights:
            copy.wait()


def entry_barrier(sizes):
    barrier = pltpu.get_barrier_semaphore()
    count = 0
    for name, size in sizes.items():
        for step in range(1, size):
            peer = lax.rem(lax.axis_index(name) + step, size)
            pl.semaphore_signal(barrier, inc=1, device_id={name: peer}, device_id_type=MESH_ID)
            count += 1
    pl.semaphore_wait(barrier, count)


def reduce_scratch(channels, sizes):
    scratch = []
    widest = max(sizes.values())
    for _, rows, order in channels:
        for name in order:
            rows //= sizes[name]
            scratch.append(pltpu.VMEM((sizes[name] - 1, rows, LANES), jnp.float32))
            scratch.append(pltpu.VMEM((rows, LANES), jnp.float32))
        for _ in range(4):
            scratch.append(pltpu.SemaphoreType.DMA((len(sizes), widest - 1)))
    return scratch


def split_scratch(channels, sizes, refs):
    phases = len(sizes)
    each = 2 * phases + 4
    recv_refs, work_refs, sems = [], [], []
    for slot in range(len(channels)):
        group = refs[slot * each : (slot + 1) * each]
        recv_refs.append(group[0 : 2 * phases : 2])
        work_refs.append(group[1 : 2 * phases : 2])
        sems.append(group[2 * phases :])
    return recv_refs, work_refs, sems


def reduce_kernel(channels, sizes, in_ref, out_ref, *scratch):
    entry_barrier(sizes)
    all_reduce_body(channels, sizes, in_ref, out_ref, *split_scratch(channels, sizes, scratch))


def all_reduce(packed, channels, sizes):
    return pl.pallas_call(
        functools.partial(reduce_kernel, channels, sizes),
        out_shape=jax.ShapeDtypeStruct(packed.shape, jnp.float32),
        in_specs=[pl.BlockSpec(memory_space=pltpu.VMEM)],
        out_specs=pl.BlockSpec(memory_space=pltpu.VMEM),
        scratch_shapes=reduce_scratch(channels, sizes),
        compiler_params=pltpu.CompilerParams(collective_id=0, has_side_effects=True, vmem_limit_bytes=24 << 20),
    )(packed)


F32 = jnp.float32
BF16 = jnp.bfloat16


def split(value):
    high = value.astype(BF16)
    return high, (value - high.astype(F32)).astype(BF16)


def product(left, right, dims):
    return lax.dot_general(left, right, (dims, ((), ())), preferred_element_type=F32)


def three_pass(left, right, dims):
    left_high, left_low = left
    right_high, right_low = right
    return (
        product(left_high, right_high, dims)
        + product(left_low, right_high, dims)
        + product(left_high, right_low, dims)
    )


LAST = ((1,), (1,))
FIRST = ((0,), (0,))
PLAIN = ((1,), (0,))


def tanh_jet(hidden, pre_slope, pre_curve):
    damping = 1.0 - hidden * hidden
    slope = damping * pre_slope
    if pre_curve is None:
        return slope, -2.0 * hidden * damping * (pre_slope * pre_slope)
    return slope, damping * pre_curve - 2.0 * hidden * damping * pre_slope * pre_slope


def tanh_jet_back(hidden, pre_slope, pre_curve, d_value, d_slope, d_curve):
    damping = 1.0 - hidden * hidden
    square = pre_slope * pre_slope
    d_pre_curve = damping * d_curve
    d_pre_slope = -4.0 * hidden * pre_slope * d_pre_curve
    bend = -2.0 * hidden * square
    if pre_curve is not None:
        bend = bend + pre_curve
    d_damping = bend * d_curve
    if d_slope is not None:
        d_pre_slope = d_pre_slope + damping * d_slope
        d_damping = d_damping + pre_slope * d_slope
    d_pre = damping * (d_value - 2.0 * square * d_pre_curve - 2.0 * hidden * d_damping)
    return d_pre, d_pre_slope, d_pre_curve


def points_column(offset, count, whole):
    position = offset + lax.broadcasted_iota(jnp.int32, (count, LANES), 0)
    return (2 * position + 1).astype(F32) * (1.0 / whole) - 1.0


def net_forward(which, points, first_row, count, refs):
    first_weight, first_bias, hidden_weight, hidden_bias, twice, bias_twice, hid, slo, cur = refs
    rows = pl.ds(first_row, count)
    weight = first_weight[which]
    hidden = jnp.tanh(points * weight + first_bias[which])
    hid[0, rows] = hidden
    slope, curve = tanh_jet(hidden, weight, None)
    depth = hidden_weight.shape[1]
    for layer in range(depth):
        stacked = jnp.dot(
            jnp.concatenate([hidden, slope, curve], 0),
            hidden_weight[which, layer],
            precision=HIGHEST,
            preferred_element_type=F32,
        )
        pre_slope = stacked[count : 2 * count]
        pre_curve = stacked[2 * count :]
        hidden = jnp.tanh(stacked[:count] + hidden_bias[which * depth + layer])
        hid[layer + 1, rows] = hidden
        slo[layer, rows] = pre_slope
        cur[layer, rows] = pre_curve
        slope, curve = tanh_jet(hidden, pre_slope, pre_curve)
    stacked = jnp.dot(
        jnp.concatenate([hidden, slope, curve], 0), twice[which], precision=HIGHEST, preferred_element_type=F32
    )
    return (
        stacked[:count] + bias_twice[which],
        stacked[count : 2 * count],
        stacked[2 * count :],
    )


def row_sum(value):
    return jnp.sum(value, 0, keepdims=True)


def net_backward(which, points, first_row, count, refs, out_ref, small, cotangents, packed, rank):
    first_weight, first_bias, hidden_weight, hidden_bias, twice, bias_twice, hid, slo, cur = refs
    depth = hidden_weight.shape[1]
    width = LANES
    rows = pl.ds(first_row, count)
    at_final = 3 * depth * width
    lane = lax.broadcasted_iota(jnp.int32, (width, 2 * rank), 1)
    low_weight = split(jnp.where(lane < rank, twice[which], 0.0))
    high_weight = split(jnp.where(lane >= rank, twice[which], 0.0)) if packed else low_weight
    hidden = hid[depth, rows]
    pre_slope = slo[depth - 1, rows]
    pre_curve = cur[depth - 1, rows]
    slope, curve = tanh_jet(hidden, pre_slope, pre_curve)
    parts = [None if cot is None else split(cot) for cot in cotangents]
    grad = three_pass(parts[0], split(hidden), FIRST)[:rank]
    curve_grad = three_pass(parts[2], split(curve), FIRST)
    grad = grad + (curve_grad[rank:] if packed else curve_grad[:rank])
    d_value = three_pass(parts[0], low_weight, LAST)
    d_curve = three_pass(parts[2], high_weight, LAST)
    d_slope = None
    if parts[1] is not None:
        grad = grad + three_pass(parts[1], split(slope), FIRST)[:rank]
        d_slope = three_pass(parts[1], low_weight, LAST)
    out_ref[pl.ds(pl.multiple_of(at_final + which * rank, 8), rank)] += grad
    biases = row_sum(cotangents[0])
    small[6 + 3 * depth + which, :, 0 : 2 * rank] += biases
    for layer in reversed(range(depth)):
        steps = tanh_jet_back(hidden, pre_slope, pre_curve, d_value, d_slope, d_curve)
        small[6 + which * depth + layer] += row_sum(steps[0])
        hidden = hid[layer, rows]
        if layer:
            pre_slope = slo[layer - 1, rows]
            pre_curve = cur[layer - 1, rows]
        else:
            pre_slope = first_weight[which]
            pre_curve = None
        slope, curve = tanh_jet(hidden, pre_slope, pre_curve)
        deltas = split(jnp.concatenate(steps, 0))
        acts = split(jnp.concatenate([hidden, slope, curve], 0))
        out_ref[pl.ds(pl.multiple_of((which * depth + layer) * width, 8), width)] += three_pass(acts, deltas, FIRST)
        back = three_pass(deltas, split(hidden_weight[which, layer]), LAST)
        d_value, d_slope, d_curve = back[:count], back[count : 2 * count], back[2 * count :]
    steps = tanh_jet_back(hidden, pre_slope, None, d_value, d_slope, d_curve)
    small[which] += row_sum(points * steps[0] + steps[1])
    small[3 + which] += row_sum(steps[0])


def step_kernel(
    wholes,
    rank,
    offsets,
    physics,
    source,
    observed,
    first_weight,
    first_bias,
    hidden_weight,
    hidden_bias,
    twice,
    bias_twice,
    out_ref,
    hid,
    slo,
    cur,
    x_rows,
    x_cols,
    y_value,
    y_both,
    y_swap,
    y_turn,
    z_first,
    z_lap,
    z_high,
    z_low,
    speed_ref,
    profile_ref,
    shape_ref,
    u_ref,
    s_ref,
    l_ref,
    f_high,
    f_low,
    x_cot,
    y_cot,
    z_turn,
    sums,
    small,
):
    refs = (first_weight, first_bias, hidden_weight, hidden_bias, twice, bias_twice, hid, slo, cur)
    x_count, y_count, z_count = source.shape
    x_whole, y_whole, z_whole = wholes
    ncells = float(x_whole * y_whole * z_whole)
    wide = 2 * rank
    out_ref[...] = jnp.zeros_like(out_ref)
    small[...] = jnp.zeros_like(small)
    y_chunks = y_count // CHUNK
    z_chunks = z_count // CHUNK
    x_base = y_count + z_count
    lane = lax.broadcasted_iota(jnp.int32, (CHUNK, wide), 1)
    low = lane < rank

    def line_points(chunk):
        on_z = chunk >= y_chunks
        first = jnp.where(on_z, offsets[2] + (chunk - y_chunks) * CHUNK, offsets[1] + chunk * CHUNK)
        scale = jnp.where(on_z, F32(1.0 / z_whole), F32(1.0 / y_whole))
        position = first + lax.broadcasted_iota(jnp.int32, (CHUNK, LANES), 0)
        return (2 * position + 1).astype(F32) * scale - 1.0

    x_points = points_column(offsets[0], x_count, x_whole)
    x_jets = net_forward(0, x_points, x_base, x_count, refs)
    for slot in range(3):
        for row in range(x_count):
            x_rows[row, :, slot * wide : (slot + 1) * wide] = x_jets[slot][row : row + 1]
    for slot in range(3):
        turned = jnp.transpose(
            jnp.concatenate([x_jets[slot], jnp.zeros((CHUNK - x_count, wide), F32)], 0)
        )
        for row in range(x_count):
            x_cols[row, slot * rank : (slot + 1) * rank] = jnp.broadcast_to(
                turned[:rank, row : row + 1], (rank, CHUNK)
            )

    def forward_chunk(chunk, carry):
        which = jnp.where(chunk >= y_chunks, 2, 1)
        start = pl.multiple_of(chunk * CHUNK, CHUNK)
        value, _, curve = net_forward(which, line_points(chunk), start, CHUNK, refs)
        both = jnp.where(low, value, curve)

        @pl.when(chunk < y_chunks)
        def _():
            rows = pl.ds(start, CHUNK)
            y_value[rows] = value
            y_both[rows] = both
            y_swap[rows] = jnp.where(low, curve, value)
            turned = jnp.transpose(both)
            for half in range(y_chunks):
                @pl.when(chunk == half)
                def _():
                    y_turn[:, half * CHUNK : (half + 1) * CHUNK] = turned

        @pl.when(chunk >= y_chunks)
        def _():
            rows = pl.ds(pl.multiple_of(start - y_count, CHUNK), CHUNK)
            value_high, value_low = split(value)
            z_first[rows, 0:wide] = value_high
            z_first[rows, wide:] = jnp.where(low, value_low.astype(F32), 0.0).astype(BF16)
            both_high, both_low = split(both)
            z_lap[rows, 0:wide] = both_high
            z_lap[rows, wide : 2 * wide] = both_high
            z_lap[rows, 2 * wide :] = both_low
            z_high[rows, 0:wide] = both_high
            z_high[rows, wide:] = both_low
            z_low[rows] = both_high

        return carry

    lax.fori_loop(0, y_chunks + z_chunks, forward_chunk, 0)

    diffusivity = jnp.exp(jnp.full((8, CHUNK), physics[0], F32))
    d_row = diffusivity[0:1]
    peak_speed = physics[1]
    bend_rate = physics[2]
    z_at = offsets[2] + lax.broadcasted_iota(jnp.int32, (1, z_count), 1)
    z_line = (2 * z_at + 1).astype(F32) * (1.0 / z_whole) - 1.0
    z_square = z_line * z_line
    tile = 16
    d_field = jnp.broadcast_to(d_row[:, 0:1], (tile, z_count))

    def plane_rows(step, carry):
        start = pl.multiple_of(step * tile, tile)
        y_at = offsets[1] + start + lax.broadcasted_iota(jnp.int32, (tile, z_count), 0)
        y_line = (2 * y_at + 1).astype(F32) * (1.0 / y_whole) - 1.0
        y_square = y_line * y_line
        base = (1.0 - y_square) * (1.0 - z_square)
        spread = y_square + z_square
        profile = base * (1.0 + bend_rate * spread)
        rows = pl.ds(start, tile)
        profile_ref[rows] = profile
        speed_ref[rows] = peak_speed * profile
        shape_ref[rows] = base * spread
        return carry

    lax.fori_loop(0, y_count // tile, plane_rows, 0)
    sums[...] = jnp.zeros_like(sums)
    y_cot[...] = jnp.zeros_like(y_cot)
    z_turn[...] = jnp.zeros_like(z_turn)
    ylow = lax.broadcasted_iota(jnp.int32, (y_count, wide), 1) < rank

    def plane(index, carry):
        value_row = x_rows[index, :, 0:wide]
        slope_row = x_rows[index, :, wide : 2 * wide]
        curve_row = x_rows[index, :, 2 * wide :]
        for scale_row, target in ((value_row, u_ref), (slope_row, s_ref)):
            high, low_part = split(y_value[...] * scale_row)
            mixed = jnp.where(ylow, high.astype(F32), low_part.astype(F32)).astype(BF16)
            target[...] = product(jnp.concatenate([mixed, high], 1), z_first[...], LAST)
        pair_lap = jnp.where(ylow, y_swap[...] * value_row + y_value[...] * curve_row, y_value[...] * value_row)
        high, low_part = split(pair_lap)
        l_ref[...] = product(jnp.concatenate([high, low_part, high], 1), z_lap[...], LAST)

        def cells(step, inner):
            start = pl.multiple_of(step * tile, tile)
            rows = pl.ds(start, tile)
            along_x = s_ref[rows]
            laplace = l_ref[rows]
            speed = speed_ref[rows]
            residual = speed * along_x - d_field * laplace - source[index, rows].astype(F32)
            misfit = u_ref[rows] - observed[index, rows].astype(F32)
            drive = residual * along_x
            sums[0] += residual * residual + misfit * misfit
            sums[1] += residual * laplace
            sums[2] += drive * profile_ref[rows]
            sums[3] += drive * shape_ref[rows]
            for slot, field in enumerate((misfit, residual * speed, residual)):
                at = pl.ds(pl.multiple_of(slot * y_count + start, tile), tile)
                f_high[at], f_low[at] = split(field)
            return inner

        lax.fori_loop(0, y_count // tile, cells, 0, unroll=2)
        over_z = product(f_high[...], z_high[...], PLAIN)
        over_z = over_z[:, :wide] + over_z[:, wide:] + product(f_low[...], z_low[...], PLAIN)
        t_m = over_z[:y_count]
        t_w = over_z[y_count : 2 * y_count]
        t_r = over_z[2 * y_count :] * (-d_row)
        t_s = jnp.concatenate([t_r[:, rank:], t_r[:, :rank]], 1)
        y_cot[0:y_count] += (
            jnp.where(ylow, value_row * t_m + slope_row * t_w + curve_row * t_r, 0.0) + value_row * t_s
        )
        y_low = y_both[...]
        x_cot[index, :, 0:wide] = row_sum(t_m * y_low)
        x_cot[index, :, wide : 2 * wide] = row_sum(t_w * y_low)
        x_cot[index, :, 2 * wide : 3 * wide] = row_sum(t_r * y_low)
        x_cot[index, :, 3 * wide :] = row_sum(t_r * y_swap[...])
        value_turn = y_turn[:rank]
        curve_turn = y_turn[rank:]
        columns = [
            jnp.concatenate([x_cols[index, slot * rank : (slot + 1) * rank]] * y_chunks, 1) for slot in range(3)
        ]
        scale = jnp.concatenate([jnp.broadcast_to(d_row, (rank, CHUNK))] * y_chunks, 1)
        pair_value = columns[0] * value_turn
        pair_curve = -scale * (columns[2] * value_turn + columns[0] * curve_turn)
        nothing = jnp.zeros((rank, y_count), F32)
        pairs = jnp.concatenate(
            [
                jnp.concatenate([pair_value, columns[1] * value_turn, pair_curve], 1),
                jnp.concatenate([nothing, nothing, -scale * pair_value], 1),
            ],
            0,
        )
        pair_high, pair_low = split(pairs)
        over_y = product(jnp.concatenate([pair_high, pair_low], 0), f_high[...], PLAIN)
        z_turn[...] += over_y[:wide] + over_y[wide:] + product(pair_high, f_low[...], PLAIN)
        return carry

    lax.fori_loop(0, x_count, plane, 0)

    factor = 2.0 / ncells
    depth = hidden_weight.shape[1]
    totals_row = 3 * depth * LANES + 3 * rank + 9 + 3 * depth
    spots = lax.broadcasted_iota(jnp.int32, (1, CHUNK), 1)
    totals = [jnp.sum(row_sum(sums[slot]), 1, keepdims=True) for slot in range(4)]
    out_ref[pl.ds(totals_row, 1), pl.ds(0, CHUNK)] = (
        jnp.where(spots == 0, totals[0] / ncells, 0.0)
        + jnp.where(spots == 1, -factor * d_row * totals[1], 0.0)
        + jnp.where(spots == 2, factor * totals[2], 0.0)
        + jnp.where(spots == 3, factor * peak_speed * totals[3], 0.0)
    )

    x_low = lax.broadcasted_iota(jnp.int32, (x_count, wide), 1) < rank
    x_cot_all = jnp.concatenate([x_cot[row] for row in range(x_count)], 0)
    mixed = x_cot_all[:, 3 * wide :]
    mixed = mixed + jnp.concatenate([mixed[:, rank:], mixed[:, :rank]], 1)
    x_cots = [
        jnp.where(x_low, factor * part, 0.0)
        for part in (x_cot_all[:, 0:wide] + mixed, x_cot_all[:, wide : 2 * wide], x_cot_all[:, 2 * wide : 3 * wide])
    ]
    net_backward(0, x_points, x_base, x_count, refs, out_ref, small, x_cots, False, rank)

    def spread_z(chunk):
        return jnp.transpose(z_turn[:, chunk * CHUNK : (chunk + 1) * CHUNK])

    for chunk in range(z_chunks):
        y_cot[y_count + chunk * CHUNK : y_count + (chunk + 1) * CHUNK] = spread_z(chunk)

    def backward_chunk(chunk, carry):
        which = jnp.where(chunk >= y_chunks, 2, 1)
        start = pl.multiple_of(chunk * CHUNK, CHUNK)
        both = factor * y_cot[pl.ds(start, CHUNK)]
        net_backward(which, line_points(chunk), start, CHUNK, refs, out_ref, small, (both, None, both), True, rank)
        return carry

    lax.fori_loop(0, y_chunks + z_chunks, backward_chunk, 0)
    at_first = 3 * depth * LANES + 3 * rank
    for slot in range(9 + 3 * depth):
        out_ref[at_first + slot : at_first + slot + 1] = small[slot]


def step_terms(offsets, wholes, padded, source, observed, physics, first_weight, first_bias, hidden_weight, hidden_bias, final_weight, final_bias):
    x_count, y_count, z_count = source.shape
    rank = final_weight.shape[2]
    depth = hidden_weight.shape[1]
    wide = 2 * rank
    lines = y_count + z_count
    vmem = pl.BlockSpec(memory_space=pltpu.VMEM)
    smem = pl.BlockSpec(memory_space=pltpu.SMEM)
    plane = pltpu.VMEM((y_count, z_count), F32)
    return pl.pallas_call(
        functools.partial(step_kernel, wholes, rank),
        out_shape=jax.ShapeDtypeStruct((padded, LANES), F32),
        in_specs=[smem, smem] + [vmem] * 8,
        out_specs=vmem,
        scratch_shapes=[
            pltpu.VMEM((depth + 1, lines + x_count, LANES), F32),
            pltpu.VMEM((depth, lines + x_count, LANES), F32),
            pltpu.VMEM((depth, lines + x_count, LANES), F32),
            pltpu.VMEM((x_count, 1, 3 * wide), F32),
            pltpu.VMEM((x_count, 3 * rank, CHUNK), F32),
            pltpu.VMEM((y_count, wide), F32),
            pltpu.VMEM((y_count, wide), F32),
            pltpu.VMEM((y_count, wide), F32),
            pltpu.VMEM((wide, y_count), F32),
            pltpu.VMEM((z_count, 2 * wide), BF16),
            pltpu.VMEM((z_count, 3 * wide), BF16),
            pltpu.VMEM((z_count, 2 * wide), BF16),
            pltpu.VMEM((z_count, wide), BF16),
            plane,
            plane,
            plane,
            plane,
            plane,
            plane,
            pltpu.VMEM((3 * y_count, z_count), BF16),
            pltpu.VMEM((3 * y_count, z_count), BF16),
            pltpu.VMEM((x_count, 1, 4 * wide), F32),
            pltpu.VMEM((lines, wide), F32),
            pltpu.VMEM((wide, z_count), F32),
            pltpu.VMEM((4, 16, z_count), F32),
            pltpu.VMEM((9 + 3 * depth, 1, LANES), F32),
        ],
        compiler_params=pltpu.CompilerParams(vmem_limit_bytes=52 << 20),
    )(
        offsets,
        physics,
        source,
        observed,
        first_weight.reshape(3, 1, LANES),
        first_bias.reshape(3, 1, LANES),
        hidden_weight,
        hidden_bias.reshape(3 * depth, 1, LANES),
        jnp.concatenate([final_weight, final_weight], 2),
        jnp.concatenate([final_bias, final_bias], 1).reshape(3, 1, wide),
    )


def local(source, observed, physics, first_weight, first_bias, hidden_weight, hidden_bias, final_weight, final_bias):
    sizes = {name: lax.axis_size(name) for name in ("gx", "gy", "gz")}
    wholes = tuple(count * size for count, size in zip(source.shape, sizes.values()))
    offsets = jnp.stack([lax.axis_index(name) * count for name, count in zip(sizes, source.shape)]).astype(jnp.int32)
    rank = final_weight.shape[2]
    depth = hidden_weight.shape[1]
    at_final = 3 * depth * LANES
    at_first = at_final + 3 * rank
    rows = at_first + 10 + 3 * depth
    padded, channels = reduce_plan(rows, sizes)
    packed = step_terms(
        offsets, wholes, padded, source, observed, physics, first_weight, first_bias,
        hidden_weight, hidden_bias, final_weight, final_bias,
    )
    summed = all_reduce(packed, channels, sizes)
    at_bias = at_first + 6 + 3 * depth
    return (
        summed[rows - 1, 0],
        summed[rows - 1, 1:4],
        summed[at_first : at_first + 3],
        summed[at_first + 3 : at_first + 6],
        summed[:at_final].reshape(hidden_weight.shape),
        summed[at_first + 6 : at_bias].reshape(hidden_bias.shape),
        jnp.swapaxes(summed[at_final:at_first].reshape(3, rank, LANES), 1, 2),
        summed[at_bias : at_bias + 3, :rank],
    )


def solution(mesh):
    in_specs = (P("gx", "gy", "gz"), P("gx", "gy", "gz"), P(), P(), P(), P(), P(), P(), P())
    out_specs = (P(), P(), P(), P(), P(), P(), P(), P())
    return jax.shard_map(local, mesh=mesh, in_specs=in_specs, out_specs=out_specs, check_vma=False)
```

profile of v0, /device:TPU:0, one launch (start us, length us, event | category | flops | bytes accessed | tf_op | source)
XLA Modules:
  0.0 92.6 jit_solution(3119976779862026942)
XLA Ops:
  0.6 0.1 pad_add_fusion.offsets
  0.7 0.8 pad_maximum_fusion.1
  1.6 0.7 reshape.37.first_weight
  2.2 0.7 reshape.38.first_bias
  2.9 0.7 reshape.39.hidden_bias
  3.6 1.1 %copy.17 = f32[3,256,64]{2,1,0:T(8,128)S(1)} copy(f32[3,256,64]{1,2,0:T(8,128)} %param.16) | data formatting | bytes 393216 | tf_op args[7]
  4.7 0.2 pad_maximum_fusion.twice
  4.9 0.0 copy-start.1
  4.9 1.4 %copy-done.1 = f32[3,2,256,256]{3,2,1,0:T(8,128)S(1)} copy-done((f32[3,2,256,256]{3,2,1,0:T(8,128)S(1)}, f32[3,2,256,256]{3,2,1,0:T(8,128)}, u32[]{:S(2)}) %copy-start.1) | copy-done | bytes 1572888
  6.3 0.0 copy-start.2
  6.3 0.7 copy-done.2
  7.0 43.0 %shard_map.152.in_ref = f32[1792,256]{1,0:T(8,128)} custom-call(s32[3]{0:T(128)S(1)} %pad_add_fusion.offsets, f32[3]{0:T(128)S(1)} %copy-done.2, bf16[8,256,512]{2,1,0:T(8,128)(2,1)} %source.1, bf16[8,256,512]{2,1,0:T(8,128)(2,1)} %observed.1, f32[3,1,256]{2,1,0:T(1,128)S(1)} %reshape.37.first_weight, f32[3,1,256]{2,1,0:T(1,128)S(1)} %reshape.38.first_bias, ...), custom_call_target="tpu_custom_call" | custom-call | tf_op jit(solution)/shard_map/pallas_call | solution.py:550
  50.0 0.0 copy-start
  50.0 1.5 %copy-done = f32[1792,256]{1,0:T(8,128)S(1)} copy-done((f32[1792,256]{1,0:T(8,128)S(1)}, f32[1792,256]{1,0:T(8,128)}, u32[]{:S(2)}) %copy-start) | copy-done | bytes 1835032
  51.5 36.3 %shard_map.153 = f32[1792,256]{1,0:T(8,128)S(1)} custom-call(f32[1792,256]{1,0:T(8,128)S(1)} %copy-done), custom_call_target="tpu_custom_call" | custom-call | tf_op jit(solution)/shard_map/pallas_call | solution.py:141
  87.8 0.5 slice.24
  88.3 0.6 slice_bitcast_fusion
  88.9 0.6 slice.31
  89.5 0.6 reshape.42
  90.1 0.6 fusion
  90.7 0.7 slice.30
  91.4 1.2 %slice.28 = f32[1536,256]{1,0:T(8,128)} slice(f32[1792,256]{1,0:T(8,128)S(1)} %shard_map.153), slice={[0:1536], [0:256]} | slice | bytes 3145728 | tf_op jit(solution)/shard_map/slice | solution.py:619
  (2 shorter events, 0.0 us)
Async XLA Ops:
  4.9 1.4 %copy-start.1 = (f32[3,2,256,256]{3,2,1,0:T(8,128)S(1)}, f32[3,2,256,256]{3,2,1,0:T(8,128)}, u32[]{:S(2)}) copy-start(f32[3,2,256,256]{3,2,1,0:T(8,128)} %hidden_weight.1) | copy-start | bytes 4718596
  6.3 0.7 copy-start.2
  50.0 1.5 %copy-start = (f32[1792,256]{1,0:T(8,128)S(1)}, f32[1792,256]{1,0:T(8,128)}, u32[]{:S(2)}) copy-start(f32[1792,256]{1,0:T(8,128)} %shard_map.152.in_ref) | copy-start | bytes 5505028
where the time goes:
time: 93 us; the launch traced here: 92.6 us
  Pallas kernels  79.3 us (85%)
  local copies, waits for them, and re-layouts  11.6 us (12%)
  other arithmetic  1.08 us (1%)
    pallas_call x1, Pallas kernels, step_terms(): pl.pallas_call(functools.partial(step_kernel, wholes, rank), out_shape=ja...  43 us
    pallas_call x1, Pallas kernels, all_reduce(): pl.pallas_call(functools.partial(reduce_kernel, channels, sizes), out_sha...  36.3 us
    unnamed x7, local copies, waits for them, and re-layouts  4.65 us

commit v1 on v0

--- a/solution.py
+++ b/solution.py
@@ -22,9 +22,12 @@
     lead = max(1, (units * 7 + 5) // 10)
     if lead == units and units > 1:
         lead -= 1
-    channels = [(0, lead * unit, ("gz", "gy", "gx"))]
+    front = (lead + 1) // 2
+    channels = [(0, front * unit, ("gz", "gy", "gx"))]
     if units > lead:
         channels.append((lead * unit, (units - lead) * unit, ("gz", "gx", "gy")))
+    if lead > front:
+        channels.append((front * unit, (lead - front) * unit, ("gz", "gy", "gx")))
     return units * unit, channels
 
 
@@ -40,60 +43,69 @@
     lengths = [rows for _, rows, _ in channels]
     bases = [first for first, _, _ in channels]
     history = [[] for _ in channels]
-    for phase in range(phases):
-        flights = []
-        for slot, (_, _, order) in enumerate(channels):
-            name = order[phase]
-            part = lengths[slot] // sizes[name]
-            for step in range(1, sizes[name]):
-                peer = lax.rem(places[name] + step, sizes[name])
-                copy = pltpu.make_async_remote_copy(
-                    src_ref=sources[slot].at[pl.ds(pl.multiple_of(starts[slot] + peer * part, 8), part)],
-                    dst_ref=recv_refs[slot][phase].at[step - 1],
-                    send_sem=sems[slot][0].at[phase, step - 1],
-                    recv_sem=sems[slot][1].at[phase, step - 1],
-                    device_id=partner(name, step),
-                    device_id_type=MESH_ID,
-                )
-                copy.start()
-                flights.append((slot, copy))
-        for slot, (_, _, order) in enumerate(channels):
-            name = order[phase]
-            part = lengths[slot] // sizes[name]
-            for owner, copy in flights:
-                if owner == slot:
-                    copy.wait()
-            mine = pl.multiple_of(starts[slot] + places[name] * part, 8)
-            value = sources[slot][pl.ds(mine, part)]
-            for step in range(1, sizes[name]):
-                value = value + recv_refs[slot][phase][step - 1]
-            history[slot].append((name, bases[slot], part))
-            bases[slot] = pl.multiple_of(bases[slot] + places[name] * part, 8)
-            if phase == phases - 1:
-                out_ref[pl.ds(bases[slot], part)] = value
-            else:
-                work_refs[slot][phase][...] = value
-                sources[slot] = work_refs[slot][phase]
-                starts[slot] = 0
-            lengths[slot] = part
-    for phase in reversed(range(phases)):
-        flights = []
+    flights = [[] for _ in channels]
+
+    def scatter(slot, phase):
+        name = channels[slot][2][phase]
+        part = lengths[slot] // sizes[name]
+        for step in range(1, sizes[name]):
+            peer = lax.rem(places[name] + step, sizes[name])
+            copy = pltpu.make_async_remote_copy(
+                src_ref=sources[slot].at[pl.ds(pl.multiple_of(starts[slot] + peer * part, 8), part)],
+                dst_ref=recv_refs[slot][phase].at[step - 1],
+                send_sem=sems[slot][0].at[phase, step - 1],
+                recv_sem=sems[slot][1].at[phase, step - 1],
+                device_id=partner(name, step),
+                device_id_type=MESH_ID,
+            )
+            copy.start()
+            flights[slot].append(copy)
+
+    def settle(slot):
+        for copy in flights[slot]:
+            copy.wait()
+        flights[slot] = []
+
+    def add_up(slot, phase):
+        name = channels[slot][2][phase]
+        part = lengths[slot] // sizes[name]
+        value = sources[slot][pl.ds(pl.multiple_of(starts[slot] + places[name] * part, 8), part)]
+        for step in range(1, sizes[name]):
+            value = value + recv_refs[slot][phase][step - 1]
+        history[slot].append((name, bases[slot], part))
+        bases[slot] = pl.multiple_of(bases[slot] + places[name] * part, 8)
+        if phase == phases - 1:
+            out_ref[pl.ds(bases[slot], part)] = value
+        else:
+            work_refs[slot][phase][...] = value
+            sources[slot] = work_refs[slot][phase]
+            starts[slot] = 0
+        lengths[slot] = part
+
+    def gather(slot, phase):
+        name, base, part = history[slot][phase]
+        mine = out_ref.at[pl.ds(pl.multiple_of(base + places[name] * part, 8), part)]
+        for step in range(1, sizes[name]):
+            copy = pltpu.make_async_remote_copy(
+                src_ref=mine,
+                dst_ref=mine,
+                send_sem=sems[slot][2].at[phase, step - 1],
+                recv_sem=sems[slot][3].at[phase, step - 1],
+                device_id=partner(name, step),
+                device_id_type=MESH_ID,
+            )
+            copy.start()
+            flights[slot].append(copy)
+
+    for turn in range(2 * phases + 1):
         for slot in range(len(channels)):
-            name, base, part = history[slot][phase]
-            mine = out_ref.at[pl.ds(pl.multiple_of(base + places[name] * part, 8), part)]
-            for step in range(1, sizes[name]):
-                copy = pltpu.make_async_remote_copy(
-                    src_ref=mine,
-                    dst_ref=mine,
-                    send_sem=sems[slot][2].at[phase, step - 1],
-                    recv_sem=sems[slot][3].at[phase, step - 1],
-                    device_id=partner(name, step),
-                    device_id_type=MESH_ID,
-                )
-                copy.start()
-                flights.append(copy)
-        for copy in flights:
-            copy.wait()
+            settle(slot)
+            if 0 < turn <= phases:
+                add_up(slot, turn - 1)
+            if turn < phases:
+                scatter(slot, turn)
+            elif turn < 2 * phases:
+                gather(slot, 2 * phases - 1 - turn)
 
 
 def entry_barrier(sizes):
@@ -293,14 +305,14 @@
     rank,
     offsets,
     physics,
-    source,
-    observed,
-    first_weight,
-    first_bias,
-    hidden_weight,
-    hidden_bias,
-    twice,
-    bias_twice,
+    source_any,
+    observed_any,
+    first_weight_in_any,
+    first_bias_in_any,
+    hidden_weight_any,
+    hidden_bias_in_any,
+    final_weight_any,
+    final_bias_any,
     out_ref,
     hid,
     slo,
@@ -328,14 +340,54 @@
     z_turn,
     sums,
     small,
+    first_weight,
+    first_bias,
+    hidden_bias,
+    twice,
+    bias_twice,
+    source,
+    observed,
+    first_weight_in,
+    first_bias_in,
+    hidden_weight,
+    hidden_bias_in,
+    final_weight,
+    final_bias,
+    arrived,
 ):
+    fetches = [
+        pltpu.make_async_copy(here, there, arrived.at[slot])
+        for slot, (here, there) in enumerate(
+            [
+                (first_weight_in_any, first_weight_in),
+                (first_bias_in_any, first_bias_in),
+                (hidden_weight_any, hidden_weight),
+                (hidden_bias_in_any, hidden_bias_in),
+                (final_weight_any, final_weight),
+                (final_bias_any, final_bias),
+                (source_any, source),
+                (observed_any, observed),
+            ]
+        )
+    ]
+    for fetch in fetches:
+        fetch.start()
+    out_ref[...] = jnp.zeros_like(out_ref)
+    small[...] = jnp.zeros_like(small)
+    for fetch in fetches[:6]:
+        fetch.wait()
     refs = (first_weight, first_bias, hidden_weight, hidden_bias, twice, bias_twice, hid, slo, cur)
+    for net in range(3):
+        first_weight[net] = first_weight_in[net : net + 1]
+        first_bias[net] = first_bias_in[net : net + 1]
+        for layer in range(hidden_weight.shape[1]):
+            hidden_bias[net * hidden_weight.shape[1] + layer] = hidden_bias_in[net, layer : layer + 1]
+        twice[net] = jnp.transpose(jnp.concatenate([final_weight[net], final_weight[net]], 0))
+        bias_twice[net] = jnp.concatenate([final_bias[net : net + 1], final_bias[net : net + 1]], 1)
     x_count, y_count, z_count = source.shape
     x_whole, y_whole, z_whole = wholes
     ncells = float(x_whole * y_whole * z_whole)
     wide = 2 * rank
-    out_ref[...] = jnp.zeros_like(out_ref)
-    small[...] = jnp.zeros_like(small)
     y_chunks = y_count // CHUNK
     z_chunks = z_count // CHUNK
     x_base = y_count + z_count
@@ -495,6 +547,8 @@
         z_turn[...] += over_y[:wide] + over_y[wide:] + product(pair_high, f_low[...], PLAIN)
         return carry
 
+    for fetch in fetches[6:]:
+        fetch.wait()
     lax.fori_loop(0, x_count, plane, 0)
 
     factor = 2.0 / ncells
@@ -550,7 +604,7 @@
     return pl.pallas_call(
         functools.partial(step_kernel, wholes, rank),
         out_shape=jax.ShapeDtypeStruct((padded, LANES), F32),
-        in_specs=[smem, smem] + [vmem] * 8,
+        in_specs=[smem, smem] + [pl.BlockSpec(memory_space=pl.ANY)] * 8,
         out_specs=vmem,
         scratch_shapes=[
             pltpu.VMEM((depth + 1, lines + x_count, LANES), F32),
@@ -579,19 +633,33 @@
             pltpu.VMEM((wide, z_count), F32),
             pltpu.VMEM((4, 16, z_count), F32),
             pltpu.VMEM((9 + 3 * depth, 1, LANES), F32),
+            pltpu.VMEM((3, 1, LANES), F32),
+            pltpu.VMEM((3, 1, LANES), F32),
+            pltpu.VMEM((3 * depth, 1, LANES), F32),
+            pltpu.VMEM((3, LANES, wide), F32),
+            pltpu.VMEM((3, 1, wide), F32),
+            pltpu.VMEM(source.shape, BF16),
+            pltpu.VMEM(observed.shape, BF16),
+            pltpu.VMEM(first_weight.shape, F32),
+            pltpu.VMEM(first_bias.shape, F32),
+            pltpu.VMEM(hidden_weight.shape, F32),
+            pltpu.VMEM(hidden_bias.shape, F32),
+            pltpu.VMEM((3, rank, LANES), F32),
+            pltpu.VMEM(final_bias.shape, F32),
+            pltpu.SemaphoreType.DMA((8,)),
         ],
-        compiler_params=pltpu.CompilerParams(vmem_limit_bytes=52 << 20),
+        compiler_params=pltpu.CompilerParams(vmem_limit_bytes=56 << 20),
     )(
         offsets,
         physics,
         source,
         observed,
-        first_weight.reshape(3, 1, LANES),
-        first_bias.reshape(3, 1, LANES),
+        first_weight,
+        first_bias,
         hidden_weight,
-        hidden_bias.reshape(3 * depth, 1, LANES),
-        jnp.concatenate([final_weight, final_weight], 2),
-        jnp.concatenate([final_bias, final_bias], 1).reshape(3, 1, wide),
+        hidden_bias,
+        jnp.swapaxes(final_weight, 1, 2),
+        final_bias,
     )
 
 

time: 93 us -> 82.1 us (0.88)
  local copies, waits for them, and re-layouts: 11.6 us -> 6.31 us
  Pallas kernels: 79.3 us -> 74.4 us
    pallas_call x1, Pallas kernels: 36.3 us -> 31.6 us  [all_reduce(): pl.pallas_call(functools.partial(reduce_kernel, channels, sizes), out_sha...]
    unnamed x7 -> x2, local copies, waits for them, and re-layouts: 4.65 us -> 1.49 us
    reshape x4 -> x0, local copies, waits for them, and re-layouts: 2.09 us -> none  [the longest x1 0.71 us: step_terms(): hidden_bias.reshape(3 * depth, 1, LANES)]
    concatenate x2 -> x0, other arithmetic: 1.01 us -> none  [the longest x1 0.83 us: step_terms(): jnp.concatenate([final_bias, final_bias], 1).reshape(3, 1, wide)]
where the time goes in v1:
time: 82.1 us; the launch traced here: 81.9 us
  Pallas kernels  74.4 us (91%)
  local copies, waits for them, and re-layouts  6.31 us (8%)
    pallas_call x1, Pallas kernels, step_terms(): pl.pallas_call(functools.partial(step_kernel, wholes, rank), out_shape=ja...  42.8 us
    pallas_call x1, Pallas kernels, all_reduce(): pl.pallas_call(functools.partial(reduce_kernel, channels, sizes), out_sha...  31.6 us

profile of v1, /device:TPU:0, one launch (start us, length us, event | category | flops | bytes accessed | tf_op | source)
XLA Modules:
  0.0 81.9 jit_solution(13755123109206397714)
XLA Ops:
  0.6 0.6 pad_add_fusion.offsets
  1.2 42.8 %shard_map.152.in_ref = f32[1792,256]{1,0:T(8,128)} custom-call(s32[3]{0:T(128)} %pad_add_fusion.offsets, f32[3]{0:T(128)} %physics.1, bf16[8,256,512]{2,1,0:T(8,128)(2,1)} %source_any.1, bf16[8,256,512]{2,1,0:T(8,128)(2,1)} %observed_any.1, f32[3,256]{1,0:T(4,128)} %first_weight_in_any.1, f32[3,256]{1,0:T(4,128)} %first_bias_in_any.1, ...), custom_call_target="tpu_custom_call" | custom-call | tf_op jit(solution)/shard_map/pallas_call | solution.py:604
  44.0 0.0 copy-start
  44.1 1.5 %copy-done = f32[1792,256]{1,0:T(8,128)S(1)} copy-done((f32[1792,256]{1,0:T(8,128)S(1)}, f32[1792,256]{1,0:T(8,128)}, u32[]{:S(2)}) %copy-start) | copy-done | bytes 1835032
  45.5 31.6 %shard_map.153 = f32[1792,256]{1,0:T(8,128)S(1)} custom-call(f32[1792,256]{1,0:T(8,128)S(1)} %copy-done), custom_call_target="tpu_custom_call" | custom-call | tf_op jit(solution)/shard_map/pallas_call | solution.py:153
  77.1 0.5 slice.24
  77.6 0.6 slice_bitcast_fusion
  78.2 0.6 slice.31
  78.8 0.6 reshape.26
  79.4 0.6 fusion
  80.0 0.7 slice.30
  80.7 1.2 %slice.28 = f32[1536,256]{1,0:T(8,128)} slice(f32[1792,256]{1,0:T(8,128)S(1)} %shard_map.153), slice={[0:1536], [0:256]} | slice | bytes 3145728 | tf_op jit(solution)/shard_map/slice | solution.py:687
  (1 shorter events, 0.0 us)
Async XLA Ops:
  44.0 1.5 %copy-start = (f32[1792,256]{1,0:T(8,128)S(1)}, f32[1792,256]{1,0:T(8,128)}, u32[]{:S(2)}) copy-start(f32[1792,256]{1,0:T(8,128)} %shard_map.152.in_ref) | copy-start | bytes 5505028
